TPU v7x, 32 devices: a whole 2x2x4 slice. The times are simulated.
32 devices in a mesh: groups: 2 (over y), chain: 4 (over x, core), sector: 4 (over z).
Axes of the slice: x: 2, y: 2, z: 4, core: 2. Of those that a mesh axis runs over, the one named last changes fastest.
Arguments:
- psi_first: bfloat16 [8, 4, 64, 1024], P(('groups', 'chain'), 'sector'), parts along dimension 0, may hold values from -6 to 6
- psi_second: bfloat16 [8, 4, 64, 1024], P(('groups', 'chain'), 'sector'), parts along dimension 0, may hold values from -6 to 6
- left_env: bfloat16 [8, 4, 64, 1664], P(('groups', 'chain'), 'sector'), parts along dimension 0, may hold values from -0.15625 to 0.15625
- right_env: bfloat16 [8, 4, 64, 1664], P(('groups', 'chain'), 'sector'), parts along dimension 0, may hold values from -0.75 to 0.75
- site_tensor: bfloat16 [8, 4, 64, 256], P(('groups', 'chain'), 'sector'), parts along dimension 0, may hold values from -3 to 3
- mpo: bfloat16 [8, 2, 26, 26, 16], P(('groups', 'chain')), parts along dimension 0, may hold values from -0.625 to 0.625
- mpo_pattern: int32 [8, 2, 26, 26], P(('groups', 'chain')), parts along dimension 0, may hold values 0 or 1
- sector_labels: int32 [8, 26, 4], P(('groups', 'chain'), None, 'sector'), parts along dimension 0, may hold values from 0 to 3, as said below
- live_sizes: int32 [8, 4], P(('groups', 'chain'), 'sector'), parts along dimension 0, may hold values from 32 to 64, as said below
Outputs:
- sigma_first: bfloat16 [8, 4, 64, 1024], P(('groups', 'chain'), 'sector'), parts along dimension 0
- sigma_second: bfloat16 [8, 4, 64, 1024], P(('groups', 'chain'), 'sector'), parts along dimension 0
- next_env: bfloat16 [8, 4, 64, 1664], P(('groups', 'chain'), 'sector'), parts along dimension 0
There are 2 independent parts, one for each index of `groups`. A program takes and returns all parts, laid end to end along the dimension named above; each array names one. Nothing has to cross between parts.
Inputs may be any that keep to these rules, and one draw needn't show every extreme that they name: `live_sizes`: in every site some sector has all 64 states live. Sector q stands at spin-up count q % (2) and spin-down count q // 2 on a periodic grid of 2 by 2 charges. Each channel x of a site carries one charge shift of 0, +1 or -1 up, +1 or -1 down (channels 0 and 25 carry 0), and sector_labels[j, x, q] is the sector at the charge of q plus that shift, wrapped on the grid.
All inputs are finite; a program needn't handle non-finite values. No bound on the sum of `mpo_pattern` on one device may be relied on, other than what follows from the above.
Results may differ from a plain program's by a relative error of at most 0.008.
Values may be sent and summed in bfloat16 or wider, within the bound.
A program may use at most 128 MiB of HBM per device.

v0:
```python
import functools

import jax
import jax.numpy as jnp
from jax import lax
from jax.experimental import pallas as pl
from jax.experimental.pallas import tpu as pltpu
from jax.sharding import PartitionSpec as P

ROWS = 32
BF16 = jnp.bfloat16
F32 = jnp.float32


def padded_operator(op, bond):
    op = jnp.transpose(op, (2, 0, 3, 1))
    op = jnp.pad(op, ((0, 0), (0, ROWS - bond), (0, 0), (0, ROWS - bond)))
    return op.reshape(op.shape[0] * ROWS, op.shape[2] * ROWS)


def halves(first, second, low):
    lane = lax.broadcasted_iota(jnp.int32, first.shape, 1)
    return jnp.where(lane < low, first, second)


def sigma_kernel(
    block, bond, local, live_ref, labels_ref, first_ref, second_ref, right_ref, left_ref, two_ref, one_ref,
    out_ref, psi_s, right_s, x_s, y_s, z_s, lk_s,
):
    wide = 2 * block
    pair = local * local
    sectors = out_ref.shape[0]
    live = live_ref[0, 0]
    row = lax.broadcasted_iota(jnp.int32, (block, wide), 0)
    lane = lax.broadcasted_iota(jnp.int32, (block, wide), 1)
    keep = (row < live) & (lax.rem(lane, block) < live)
    for tile in range(pair // 2):
        at = slice(tile * wide, (tile + 1) * wide)
        a = first_ref[:, at].astype(F32)
        b = second_ref[:, at].astype(F32)
        even = jnp.where(lane < block, a, pltpu.roll(b, block, 1))
        odd = jnp.where(lane < block, pltpu.roll(a, block, 1), b)
        psi_s[pl.ds(2 * tile * block, block), :] = jnp.where(keep, even, 0.0).astype(BF16)
        psi_s[pl.ds((2 * tile + 1) * block, block), :] = jnp.where(keep, odd, 0.0).astype(BF16)
    for tile in range(bond // 2):
        a = right_ref[:, tile * wide : (tile + 1) * wide].astype(F32)
        swapped = pltpu.roll(a, block, 1)
        zero = jnp.zeros_like(a)
        right_s[pl.ds(tile * 2 * wide, block), :] = jnp.where(lane < block, a, zero).astype(BF16)
        right_s[pl.ds(tile * 2 * wide + block, block), :] = jnp.where(lane < block, zero, swapped).astype(BF16)
        right_s[pl.ds(tile * 2 * wide + wide, block), :] = jnp.where(lane < block, swapped, zero).astype(BF16)
        right_s[pl.ds(tile * 2 * wide + wide + block, block), :] = jnp.where(lane < block, zero, a).astype(BF16)
    for k in range(sectors):
        lk_s[pl.ds(k * block, block), :] = jnp.where(
            labels_ref[...] == k, left_ref[...].astype(F32), 0.0
        ).astype(BF16)
    stride = pair * ROWS

    def put(st, w, value):
        x_s[pl.ds(st * ROWS + w, block, stride=stride), :] = value

    for st in range(pair):
        for w in range(bond, ROWS):
            put(st, w, jnp.zeros((block, wide), F32))

    def one(st, carry):
        lhs = psi_s[pl.ds(pl.multiple_of(st * block, block), block), :]
        for tile in range(bond // 2):
            got = lax.dot_general(
                lhs, right_s[pl.ds(tile * 2 * wide, 2 * wide), :], (((1,), (1,)), ((), ())),
                preferred_element_type=F32,
            )
            put(st, 2 * tile, got[:, :wide])
            put(st, 2 * tile + 1, got[:, wide:])
        return carry

    lax.fori_loop(0, pair, one, 0)
    two = two_ref[...]
    rows = local * ROWS

    def middle(a, carry):
        x = x_s[pl.ds(pl.multiple_of(a * stride, stride), stride), :].astype(BF16)
        x = jnp.concatenate([x[s * rows : (s + 1) * rows] for s in range(local)], axis=1)
        y = jnp.dot(two, x, preferred_element_type=F32).astype(BF16)
        for u in range(local):
            for s in range(local):
                y_s[u, pl.ds(pl.multiple_of(a * rows, rows) + s * ROWS, ROWS), :] = y[
                    u * ROWS : (u + 1) * ROWS, s * wide : (s + 1) * wide
                ]
        return carry

    lax.fori_loop(0, block, middle, 0, unroll=2)
    op = one_ref[...]
    group = 4

    def last(u, carry):
        def third(step, carry):
            y = y_s[u, pl.ds(pl.multiple_of(step * group * rows, group * rows), group * rows), :]
            y = jnp.concatenate([y[g * rows : (g + 1) * rows] for g in range(group)], axis=1)
            z = jnp.dot(op, y, preferred_element_type=F32).astype(BF16)
            for g in range(group):
                for r in range(local):
                    z_s[pl.ds(pl.multiple_of(step * group * ROWS, group * ROWS) + g * ROWS, ROWS), r * wide : (r + 1) * wide] = z[
                        r * ROWS : (r + 1) * ROWS, g * wide : (g + 1) * wide
                    ]
            return carry

        lax.fori_loop(0, block // group, third, 0, unroll=2)
        half = local * wide // 2
        for part in range(2):
            got = jnp.dot(lk_s[...], z_s[:, part * half : (part + 1) * half], preferred_element_type=F32)
            out_ref[:, u, :, part * half : (part + 1) * half] = got.astype(BF16).reshape(sectors, block, half)
        return carry

    lax.fori_loop(0, local, last, 0)


def sigma_partial(live, labels, first, second, right, left, two, one, sectors, bond):
    block = first.shape[0]
    local = two.shape[0] // ROWS
    wide = 2 * block
    pair = local * local
    vmem = pl.BlockSpec(memory_space=pltpu.VMEM)
    return pl.pallas_call(
        functools.partial(sigma_kernel, block, bond, local),
        out_shape=jax.ShapeDtypeStruct((sectors, local, block, local * wide), BF16),
        in_specs=[pl.BlockSpec(memory_space=pltpu.SMEM)] + [vmem] * 7,
        out_specs=vmem,
        scratch_shapes=[
            pltpu.VMEM((pair * block, wide), BF16),
            pltpu.VMEM((bond * wide, wide), BF16),
            pltpu.VMEM((block * pair * ROWS, wide), F32),
            pltpu.VMEM((local, block * local * ROWS, wide), BF16),
            pltpu.VMEM((block * ROWS, local * wide), BF16),
            pltpu.VMEM((sectors * block, block * ROWS), BF16),
        ],
        compiler_params=pltpu.CompilerParams(vmem_limit_bytes=56 * 1024 * 1024),
    )(live, labels, first, second, right, left, two, one)


def shards(
    psi_first, psi_second, left_env, right_env, site_tensor, mpo, mpo_pattern, sector_labels, live_sizes,
):
    block_size = psi_first.shape[2]
    mpo_bond = mpo.shape[2]
    physical = site_tensor.shape[3] // block_size
    sectors = lax.axis_size("sector")
    kept = (jnp.arange(block_size, dtype=jnp.int32)[None, :] < live_sizes[0][:, None]).astype(BF16)
    masked = (mpo[0] * mpo_pattern[0][..., None].astype(BF16)).reshape(
        2, mpo_bond, mpo_bond, physical, physical
    )
    labels = sector_labels[0]
    one = padded_operator(masked[0], mpo_bond)
    two = padded_operator(masked[1], mpo_bond)
    left_t = jnp.pad(
        jnp.transpose(left_env[0, 0].reshape(block_size, mpo_bond, block_size), (0, 2, 1)),
        ((0, 0), (0, 0), (0, ROWS - mpo_bond)),
    ).reshape(block_size, block_size * ROWS)
    labels_row = jnp.tile(jnp.pad(labels[:, 0], (0, ROWS - mpo_bond), constant_values=-1), block_size)[None]
    partial = sigma_partial(
        live_sizes, labels_row, psi_first[0, 0], psi_second[0, 0], right_env[0, 0], left_t, two, one,
        sectors, mpo_bond,
    )
    site_part = (
        site_tensor[0].reshape(1, block_size, physical, block_size)
        * kept[:, :, None, None]
        * kept[:, None, None, :]
    )
    gathered = lax.all_gather(site_part, "sector", axis=0, tiled=True)
    left_part = left_env[0].reshape(1, block_size, mpo_bond, block_size)
    env_one = jnp.einsum("qbwa,qasc->qwbsc", left_part, site_part, preferred_element_type=F32).astype(BF16)
    bra = jnp.take(gathered, jnp.transpose(labels), axis=0)
    env_two = jnp.einsum("qwbre,qwbsc->qwresc", bra, env_one, preferred_element_type=F32).astype(BF16)
    updated = jnp.einsum("wvrs,qwresc->qevc", masked[0], env_two, preferred_element_type=F32).astype(BF16)
    updated = updated.reshape(1, 1, block_size, mpo_bond * block_size)
    count = lax.axis_size("chain")
    received = lax.ppermute(updated, "chain", [(i, i + 1) for i in range(count - 1)])
    next_env = jnp.where(lax.axis_index("chain") == 0, left_env, received)
    owned = lax.psum_scatter(partial, "sector", scatter_dimension=0, tiled=True)[0]
    owned = owned.reshape(physical, block_size, physical, 2, block_size).astype(F32)
    owned = owned * kept[0].astype(F32)[None, :, None, None, None] * kept[0].astype(F32)
    sigmas = jnp.transpose(owned, (3, 1, 2, 0, 4)).astype(BF16).reshape(2, 1, 1, block_size, -1)
    return (sigmas[0], sigmas[1], next_env)


def solution(mesh):
    return jax.shard_map(
        shards,
        mesh=mesh,
        in_specs=(
            P(("groups", "chain"), "sector", None, None),
            P(("groups", "chain"), "sector", None, None),
            P(("groups", "chain"), "sector", None, None),
            P(("groups", "chain"), "sector", None, None),
            P(("groups", "chain"), "sector", None, None),
            P(("groups", "chain"), None, None, None, None),
            P(("groups", "chain"), None, None, None),
            P(("groups", "chain"), None, "sector"),
            P(("groups", "chain"), "sector"),
        ),
        out_specs=(
            P(("groups", "chain"), "sector", None, None),
            P(("groups", "chain"), "sector", None, None),
            P(("groups", "chain"), "sector", None, None),
        ),
        check_vma=False,
    )
```

profile of v0, /device:TPU:14, one launch (start us, length us, event | category | flops | bytes accessed | tf_op | source)
XLA Modules:
  0.0 99.5 jit_solution(6416539235114744554)
XLA Ops:
  7.9 0.7 pad.15
  8.5 0.7 broadcast_in_dim_tile.3.labels_ref
  9.2 1.4 %reshape_squeeze.8 = bf16[64,26,64]{2,1,0:T(8,128)(2,1)S(1)} reshape(bf16[1,1,64,1664]{3,2,1,0:T(8,128)(2,1)} %param.11) | data formatting | bytes 425984 | tf_op jit(solution)/shard_map/reshape;squeeze | solution.py:156
  10.6 1.1 %copy.67 = bf16[64,64,26]{0,2,1:T(8,128)(2,1)S(1)} copy(bf16[64,64,26]{1,2,0:T(8,128)(2,1)S(1)} %bitcast.68) | data formatting | bytes 425984
  11.7 0.1 pad.16.clone
  11.8 0.9 copy.49.left_ref
  13.0 0.7 reshape.132.two_ref
  13.7 0.2 copy.47
  13.9 0.2 copy.68
  14.3 0.7 reshape.133.one_ref
  15.0 35.2 %shard_map.112 = bf16[4,4,64,512]{3,2,1,0:T(8,128)(2,1)} custom-call(s32[1,1]{1,0:T(1,128)} %copy.85.live_ref, s32[1,2048]{1,0:T(1,128)} %broadcast_in_dim_tile.3.labels_ref, bf16[64,1024]{1,0:T(8,128)(2,1)} %bitcast.76, bf16[64,1024]{1,0:T(8,128)(2,1)} %bitcast.77, bf16[64,1664]{1,0:T(8,128)(2,1)} %bitcast.75, bf16[64,2048]{1,0:T(8,128)(2,1)} %copy.49.left_ref, ...), custom_call_target="tpu_custom_call" | custom-call | tf_op jit(solution)/shard_map/pallas_call | solution.py:124
  50.3 0.1 mul.87
  50.4 0.1 reshape_squeeze.9
  50.5 0.1 multiply_multiply_fusion.1
  50.6 0.1 copy.64
  50.7 0.6 fusion.6
  51.3 0.1 multiply_multiply_fusion
  51.5 16.4 %all_gather.3 = bf16[4,64,4,64]{3,1,2,0:T(8,128)(2,1)S(1)} all-gather(bf16[1,64,4,64]{3,1,2,0:T(8,128)(2,1)S(1)} %copy.52), channel_id=1, replica_groups=mesh['groups'=2,'chain'=4,'sector'=4] {'sector'}, dimensions={0}, use_global_device_ids=true | all-gather | bytes 163840 | tf_op jit(solution)/shard_map/all_gather | solution.py:169
  67.9 2.0 %gather_fusion = bf16[26,64,4,64]{3,1,2,0:T(8,128)(2,1)} fusion(bf16[4,64,4,64]{3,1,2,0:T(8,128)(2,1)S(1)} %all_gather.3, s32[1024]{0:T(1024)S(1)} %pad_clamp_fusion), kind=kCustom, calls=%fused_computation | custom fusion | bytes 1704040 | tf_op jit(solution)/shard_map/jit(_take)/gather | solution.py:172
  69.9 5.0 %convolution_convert_fusion = bf16[26,4,64,4,64]{4,2,3,1,0:T(8,128)(2,1)S(1)} fusion(bf16[26,64,4,64,1]{1,3,0,2,4:T(8,128)(2,1)S(1)} %fusion.6, bf16[26,64,4,64]{3,1,2,0:T(8,128)(2,1)} %gather_fusion, pred[26]{0:T(512)(128)(4,1)S(1)} %and_bitcast_fusion), kind=kOutput, calls=%fused_computation.3 | convolution fusion | flops 220233728 | bytes 5111834 | tf_op jit(solution)/shard_map/qwbre,qwbsc->qwresc/dot_general | solution.py:173
  75.0 3.9 %fusion.13 = bf16[1,64,26,64]{3,2,1,0:T(8,128)(2,1)S(1)} fusion(bf16[26,26,4,4,1]{0,1,3,2,4:T(8,128)(2,1)S(1)} %bitcast.71, bf16[26,4,64,4,64]{4,2,3,1,0:T(8,128)(2,1)S(1)} %convolution_convert_fusion), kind=kOutput, calls=%fused_computation.12 | convolution fusion | flops 88711168 | bytes 3642496 | tf_op jit(solution)/shard_map/wvrs,qwresc->qevc/dot_general | solution.py:174
  78.9 0.4 reshape.135
  79.3 1.9 %collective-permute-start = (bf16[1,1,64,1664]{3,2,1,0:T(8,128)(2,1)S(1)}, bf16[1,1,64,1664]{3,2,1,0:T(8,128)(2,1)S(1)}, u32[]{:S(2)}, u32[]{:S(2)}) collective-permute-start(bf16[1,1,64,1664]{3,2,1,0:T(8,128)(2,1)S(1)} %reshape.135), channel_id=1, source_target_pairs={{0,4},{4,8},{8,12},{1,5},{5,9},{9,13},{2,6},{6,10},{10,14},{3,7},{... | collective-permute-start | bytes 638984 | tf_op jit(solution)/shard_map/ppermute | solution.py:177
  81.3 5.2 %collective-permute-done = bf16[1,1,64,1664]{3,2,1,0:T(8,128)(2,1)S(1)} collective-permute-done((bf16[1,1,64,1664]{3,2,1,0:T(8,128)(2,1)S(1)}, bf16[1,1,64,1664]{3,2,1,0:T(8,128)(2,1)S(1)}, u32[]{:S(2)}, u32[]{:S(2)}) %collective-permute-start) | collective-permute-done | bytes 213024 | tf_op jit(solution)/shard_map/ppermute | solution.py:177
  86.5 0.7 broadcast_select_fusion
  87.2 1.7 %reshape.136 = f32[4,64,4,2,64]{4,3,2,1,0:T(2,128)S(1)} reshape(bf16[1,4,64,512]{3,2,1,0:T(8,128)(2,1)} %reduce-scatter.2.cloned.1.call-done) | data formatting | bytes 786432 | tf_op jit(solution)/shard_map/convert_element_type | solution.py:180
  88.9 0.5 fusion.17
  89.5 0.7 fusion.23
  90.2 0.3 copy.50
  90.6 0.9 squeeze.33
  91.4 0.3 copy.51
  91.8 0.9 squeeze.34
  (27 shorter events, 0.4 us)
Async XLA Ops:
  7.2 80.0 %reduce-scatter.2.cloned.1.call-start = ((), (), s32[]{:S(2)}) async-start(), calls=%async_computation.1 | async-start | bytes 1310720 | tf_op jit(solution)/shard_map/reduce_scatter | solution.py:179
  9.2 3.5 %copy-start.3 = (s32[1,2,26,26]{3,1,2,0:T(2,128)S(1)}, s32[1,2,26,26]{3,1,2,0:T(2,128)}, u32[]{:S(2)}) copy-start(s32[1,2,26,26]{3,1,2,0:T(2,128)} %param.15) | copy-start | bytes 16228
  9.2 3.6 %copy-start.1 = (bf16[1,2,26,26,16]{3,4,2,1,0:T(8,128)(2,1)S(1)}, bf16[1,2,26,26,16]{3,4,2,1,0:T(8,128)(2,1)}, u32[]{:S(2)}) copy-start(bf16[1,2,26,26,16]{3,4,2,1,0:T(8,128)(2,1)} %param.14) | copy-start | bytes 129796
  14.2 36.1 %copy-start.4 = (s32[1,26,1]{1,2,0:T(1,128)S(1)}, s32[1,26,1]{1,2,0:T(1,128)}, u32[]{:S(2)}) copy-start(s32[1,26,1]{1,2,0:T(1,128)} %param.16) | copy-start | bytes 316
  14.2 36.2 %copy-start.2 = (bf16[1,1,64,256]{3,2,1,0:T(8,128)(2,1)S(1)}, bf16[1,1,64,256]{3,2,1,0:T(8,128)(2,1)}, u32[]{:S(2)}) copy-start(bf16[1,1,64,256]{3,2,1,0:T(8,128)(2,1)} %param.13) | copy-start | bytes 98308
  74.9 11.5 %copy-start = (bf16[1,1,64,1664]{3,2,1,0:T(8,128)(2,1)S(1)}, bf16[1,1,64,1664]{3,2,1,0:T(8,128)(2,1)}, u32[]{:S(2)}) copy-start(bf16[1,1,64,1664]{3,2,1,0:T(8,128)(2,1)} %param.11) | copy-start | bytes 638980
  79.3 7.2 %collective-permute-start = (bf16[1,1,64,1664]{3,2,1,0:T(8,128)(2,1)S(1)}, bf16[1,1,64,1664]{3,2,1,0:T(8,128)(2,1)S(1)}, u32[]{:S(2)}, u32[]{:S(2)}) collective-permute-start(bf16[1,1,64,1664]{3,2,1,0:T(8,128)(2,1)S(1)} %reshape.135), channel_id=1, source_target_pairs={{0,4},{4,8},{8,12},{1,5},{5,9},{9,13},{2,6},{6,10},{10,14},{3,7},{... | collective-permute-start | bytes 638984 | tf_op jit(solution)/shard_map/ppermute | solution.py:177
Sparse Core Ops, SparseCore 0:
  50.4 28.4 reduce-scatter.1
where the time goes:
time: 99.7 us; the launch traced here: 99.5 us
  Pallas kernels  35.2 us (35%)
  blocking collectives  16.4 us (16%)
  between operations  14.9 us (15%)
  local copies, waits for them, and re-layouts  14.6 us (15%)
  matrix products  9.59 us (10%)
  waiting for transfers between devices  5.25 us (5%)
  starting transfers between devices  1.96 us (2%)
  other arithmetic  1.52 us (2%)
    pallas_call x1, Pallas kernels, sigma_partial(): pl.pallas_call(functools.partial(sigma_kernel, block, bond, local), out_s...  35.2 us
    all_gather x1, blocking collectives, shards(): gathered = lax.all_gather(site_part, 'sector', axis=0, tiled=True)  16.4 us
    ppermute x1, waiting for transfers between devices, shards(): lax.ppermute(updated, 'chain', [(i, i + 1) for i in range(count - 1)])  5.23 us
    dot_general x1, matrix products, shards(): jnp.einsum('qwbre,qwbsc->qwresc', bra, env_one, preferred_element_type=F32)  4.99 us
    dot_general x1, matrix products, shards(): jnp.einsum('wvrs,qwresc->qevc', masked[0], env_two, preferred_element_typ...  3.95 us
    gather x1, local copies, waits for them, and re-layouts, shards(): bra = jnp.take(gathered, jnp.transpose(labels), axis=0)  2.02 us
  transfers between devices with their start and end apart: 2, of which 1 were waited for; matrix products, arithmetic and copies ran while one was open for 13% of the time, Pallas kernels for 0%

commit v1 on v0

v1 whole, which is shorter than its diff:
```python
import functools

import jax
import jax.numpy as jnp
from jax import lax
from jax.experimental import pallas as pl
from jax.experimental.pallas import tpu as pltpu
from jax.sharding import PartitionSpec as P

ROWS = 32
BF16 = jnp.bfloat16
F32 = jnp.float32
MESH = pl.DeviceIdType.MESH


def padded_operator(op, bond):
    op = jnp.transpose(op, (2, 0, 3, 1))
    op = jnp.pad(op, ((0, 0), (0, ROWS - bond), (0, 0), (0, ROWS - bond)))
    return op.reshape(op.shape[0] * ROWS, op.shape[2] * ROWS)


def window_kernel(
    block, bond, local, sectors, segments,
    live_ref, labels_ref, first_ref, second_ref, left_ref, right_ref, site_ref, left_t_ref, two_ref, one_ref,
    out_first_ref, out_second_ref, out_env_ref,
    psi_s, right_s, x_s, y_s, z_s, lk_s, site_s, site_t, v_s, sum_s, got_s, env_s, env_got,
    site_send, site_recv, sum_send, sum_recv, env_send, env_recv,
):
    me = lax.axis_index("sector")
    segment = lax.axis_index("chain")
    barrier = pltpu.get_barrier_semaphore()
    peers = [lax.rem(me + j, sectors) for j in range(1, sectors)]
    for peer in peers:
        pl.semaphore_signal(barrier, inc=1, device_id={"sector": peer}, device_id_type=MESH)

    @pl.when(segment > 0)
    def _():
        pl.semaphore_signal(barrier, inc=1, device_id={"chain": segment - 1}, device_id_type=MESH)

    @pl.when(segment < segments - 1)
    def _():
        pl.semaphore_signal(barrier, inc=1, device_id={"chain": segment + 1}, device_id_type=MESH)

    waits = sectors - 1 + jnp.where(segment > 0, 1, 0) + jnp.where(segment < segments - 1, 1, 0)
    pl.semaphore_wait(barrier, waits)

    wide = 2 * block
    pair = local * local
    live = live_ref[0, 0]
    low = lax.broadcasted_iota(jnp.int32, (block, local * block), 0) < live
    low = low & (lax.rem(lax.broadcasted_iota(jnp.int32, (block, local * block), 1), block) < live)
    site_s[me] = jnp.where(low, site_ref[...].astype(F32), 0.0).astype(BF16)

    def site_copy(j):
        return pltpu.make_async_remote_copy(
            src_ref=site_s.at[me], dst_ref=site_s.at[me], send_sem=site_send.at[j - 1],
            recv_sem=site_recv.at[j - 1], device_id={"sector": peers[j - 1]}, device_id_type=MESH,
        )

    for j in range(1, sectors):
        site_copy(j).start()
    row = lax.broadcasted_iota(jnp.int32, (block, wide), 0)
    lane = lax.broadcasted_iota(jnp.int32, (block, wide), 1)
    keep = (row < live) & (lax.rem(lane, block) < live)
    for tile in range(pair // 2):
        at = slice(tile * wide, (tile + 1) * wide)
        a = first_ref[:, at].astype(F32)
        b = second_ref[:, at].astype(F32)
        even = jnp.where(lane < block, a, pltpu.roll(b, block, 1))
        odd = jnp.where(lane < block, pltpu.roll(a, block, 1), b)
        psi_s[pl.ds(2 * tile * block, block), :] = jnp.where(keep, even, 0.0).astype(BF16)
        psi_s[pl.ds((2 * tile + 1) * block, block), :] = jnp.where(keep, odd, 0.0).astype(BF16)
    for tile in range(bond // 2):
        a = right_ref[:, tile * wide : (tile + 1) * wide].astype(F32)
        swapped = pltpu.roll(a, block, 1)
        zero = jnp.zeros_like(a)
        right_s[pl.ds(tile * 2 * wide, block), :] = jnp.where(lane < block, a, zero).astype(BF16)
        right_s[pl.ds(tile * 2 * wide + block, block), :] = jnp.where(lane < block, zero, swapped).astype(BF16)
        right_s[pl.ds(tile * 2 * wide + wide, block), :] = jnp.where(lane < block, swapped, zero).astype(BF16)
        right_s[pl.ds(tile * 2 * wide + wide + block, block), :] = jnp.where(lane < block, zero, a).astype(BF16)
    row_lane = lax.rem(lax.broadcasted_iota(jnp.int32, (block, wide), 1), ROWS)
    target = jnp.full((block, wide), -1, jnp.int32)
    for w in range(bond):
        target = jnp.where(row_lane == w, labels_ref[w, 0], target)
    for tile in range(block * ROWS // wide):
        at = slice(tile * wide, (tile + 1) * wide)
        a = left_t_ref[:, at].astype(F32)
        for k in range(sectors):
            lk_s[k * block : (k + 1) * block, at] = jnp.where(target == k, a, 0.0).astype(BF16)
    stride = pair * ROWS

    def put(st, w, value):
        x_s[pl.ds(st * ROWS + w, block, stride=stride), :] = value

    for st in range(pair):
        for w in range(bond, ROWS):
            put(st, w, jnp.zeros((block, wide), F32))

    def one(st, carry):
        lhs = psi_s[pl.ds(pl.multiple_of(st * block, block), block), :]
        for tile in range(bond // 2):
            got = lax.dot_general(
                lhs, right_s[pl.ds(tile * 2 * wide, 2 * wide), :], (((1,), (1,)), ((), ())),
                preferred_element_type=F32,
            )
            put(st, 2 * tile, got[:, :wide])
            put(st, 2 * tile + 1, got[:, wide:])
        return carry

    lax.fori_loop(0, pair, one, 0)
    two = two_ref[...]
    rows = local * ROWS

    def middle(a, carry):
        x = x_s[pl.ds(pl.multiple_of(a * stride, stride), stride), :].astype(BF16)
        x = jnp.concatenate([x[s * rows : (s + 1) * rows] for s in range(local)], axis=1)
        y = jnp.dot(two, x, preferred_element_type=F32).astype(BF16)
        for u in range(local):
            for s in range(local):
                y_s[u, pl.ds(pl.multiple_of(a * rows, rows) + s * ROWS, ROWS), :] = y[
                    u * ROWS : (u + 1) * ROWS, s * wide : (s + 1) * wide
                ]
        return carry

    lax.fori_loop(0, block, middle, 0, unroll=2)
    op = one_ref[...]
    group = 4

    def sum_copy(j, u):
        return pltpu.make_async_remote_copy(
            src_ref=sum_s.at[peers[j - 1], u], dst_ref=got_s.at[j - 1, u], send_sem=sum_send.at[j - 1, u],
            recv_sem=sum_recv.at[j - 1, u], device_id={"sector": peers[j - 1]}, device_id_type=MESH,
        )

    def last(u, carry):
        def third(step, carry):
            y = y_s[u, pl.ds(pl.multiple_of(step * group * rows, group * rows), group * rows), :]
            y = jnp.concatenate([y[g * rows : (g + 1) * rows] for g in range(group)], axis=1)
            z = jnp.dot(op, y, preferred_element_type=F32).astype(BF16)
            for g in range(group):
                for r in range(local):
                    z_s[pl.ds(pl.multiple_of(step * group * ROWS, group * ROWS) + g * ROWS, ROWS), r * wide : (r + 1) * wide] = z[
                        r * ROWS : (r + 1) * ROWS, g * wide : (g + 1) * wide
                    ]
            return carry

        lax.fori_loop(0, block // group, third, 0, unroll=2)
        half = local * wide // 2
        for part in range(2):
            got = jnp.dot(lk_s[...], z_s[:, part * half : (part + 1) * half], preferred_element_type=F32)
            sum_s[:, u, :, part * half : (part + 1) * half] = got.astype(BF16).reshape(sectors, block, half)
        for j in range(1, sectors):
            sum_copy(j, u).start()
        return carry

    lax.fori_loop(0, local, last, 0)

    for j in range(1, sectors):
        site_copy(j).wait()
    for q in range(sectors):
        site_t[q] = site_s[q].astype(F32).T.astype(BF16)
    own = site_s[me]
    own = jnp.concatenate([own, own], axis=0)
    op_t = op.astype(F32).T.astype(BF16)
    tiles = local * block // wide
    env_stride = tiles * rows

    def brought(tile, carry):
        a = left_ref[:, pl.ds(pl.multiple_of(tile * wide, wide), wide)].astype(F32)
        for odd in range(2):
            w = 2 * tile + odd
            part = jnp.where((lane >= block) if odd else (lane < block), a, 0.0).astype(BF16)
            e_one = jnp.dot(part, own, preferred_element_type=F32).astype(BF16)
            e_two = jnp.dot(site_t[labels_ref[w, 0]], e_one, preferred_element_type=F32)
            for t in range(tiles):
                for r in range(local):
                    x_s[pl.ds(t * rows + r * ROWS + w, block, stride=env_stride), :] = e_two[
                        r * block : (r + 1) * block, t * wide : (t + 1) * wide
                    ]
        return carry

    lax.fori_loop(0, bond // 2, brought, 0)

    def closed(e, carry):
        x = x_s[pl.ds(pl.multiple_of(e * env_stride, env_stride), env_stride), :].astype(BF16)
        x = jnp.concatenate([x[t * rows : (t + 1) * rows] for t in range(tiles)], axis=1)
        o = jnp.dot(op_t, x, preferred_element_type=F32)
        even = o[:ROWS, :wide]
        odd = o[ROWS : 2 * ROWS, :wide]
        for t in range(1, tiles):
            even = even + o[2 * t * ROWS : (2 * t + 1) * ROWS, t * wide : (t + 1) * wide]
            odd = odd + o[(2 * t + 1) * ROWS : (2 * t + 2) * ROWS, t * wide : (t + 1) * wide]
        v_s[pl.ds(e, ROWS, stride=block), :] = even + pltpu.roll(odd, block, 1)
        return carry

    lax.fori_loop(0, block, closed, 0, unroll=4)
    for tile in range(bond // 2):
        a = v_s[2 * tile * block : (2 * tile + 1) * block, :]
        b = v_s[(2 * tile + 1) * block : (2 * tile + 2) * block, :]
        env_s[:, tile * wide : (tile + 1) * wide] = jnp.where(lane < block, a, pltpu.roll(b, block, 1)).astype(BF16)

    def env_copy():
        return pltpu.make_async_remote_copy(
            src_ref=env_s, dst_ref=env_got, send_sem=env_send, recv_sem=env_recv,
            device_id={"chain": jnp.minimum(segment + 1, segments - 1)}, device_id_type=MESH,
        )

    @pl.when(segment < segments - 1)
    def _():
        env_copy().start()

    for u in range(0, local, 2):
        for j in range(1, sectors):
            sum_copy(j, u).wait()
            sum_copy(j, u + 1).wait()
        for r in range(local):
            at = slice(r * wide, (r + 1) * wide)
            total = []
            for v in range(2):
                t = sum_s[me, u + v, :, at].astype(F32)
                for j in range(sectors - 1):
                    t = t + got_s[j, u + v, :, at].astype(F32)
                total.append(jnp.where(keep, t, 0.0))
            a, b = total
            to = slice((r * local + u) * block, (r * local + u + 2) * block)
            out_first_ref[:, to] = jnp.where(lane < block, a, pltpu.roll(b, block, 1)).astype(BF16)
            out_second_ref[:, to] = jnp.where(lane < block, pltpu.roll(a, block, 1), b).astype(BF16)

    @pl.when(segment < segments - 1)
    def _():
        env_copy().wait_send()

    @pl.when(segment > 0)
    def _():
        env_copy().wait_recv()
        out_env_ref[...] = env_got[...]

    @pl.when(segment == 0)
    def _():
        out_env_ref[...] = left_ref[...]


def shards(
    psi_first, psi_second, left_env, right_env, site_tensor, mpo, mpo_pattern, sector_labels, live_sizes,
):
    block = psi_first.shape[2]
    bond = mpo.shape[2]
    local = site_tensor.shape[3] // block
    sectors = lax.axis_size("sector")
    segments = lax.axis_size("chain")
    wide = 2 * block
    pair = local * local
    masked = (mpo[0] * mpo_pattern[0][..., None].astype(BF16)).reshape(2, bond, bond, local, local)
    one = padded_operator(masked[0], bond)
    two = padded_operator(masked[1], bond)
    left = left_env[0, 0]
    left_t = jnp.pad(
        jnp.transpose(left.reshape(block, bond, block), (0, 2, 1)), ((0, 0), (0, 0), (0, ROWS - bond))
    ).reshape(block, block * ROWS)
    vmem = pl.BlockSpec(memory_space=pltpu.VMEM)
    smem = pl.BlockSpec(memory_space=pltpu.SMEM)
    outs = pl.pallas_call(
        functools.partial(window_kernel, block, bond, local, sectors, segments),
        out_shape=(
            jax.ShapeDtypeStruct((block, pair * block), BF16),
            jax.ShapeDtypeStruct((block, pair * block), BF16),
            jax.ShapeDtypeStruct((block, bond * block), BF16),
        ),
        in_specs=[smem] * 2 + [vmem] * 8,
        out_specs=(vmem,) * 3,
        scratch_shapes=[
            pltpu.VMEM((pair * block, wide), BF16),
            pltpu.VMEM((bond * wide, wide), BF16),
            pltpu.VMEM((block * pair * ROWS, wide), F32),
            pltpu.VMEM((local, block * local * ROWS, wide), BF16),
            pltpu.VMEM((block * ROWS, local * wide), BF16),
            pltpu.VMEM((sectors * block, block * ROWS), BF16),
            pltpu.VMEM((sectors, block, local * block), BF16),
            pltpu.VMEM((sectors, local * block, block), BF16),
            pltpu.VMEM((ROWS * block, wide), F32),
            pltpu.VMEM((sectors, local, block, local * wide), BF16),
            pltpu.VMEM((sectors - 1, local, block, local * wide), BF16),
            pltpu.VMEM((block, bond * block), BF16),
            pltpu.VMEM((block, bond * block), BF16),
            pltpu.SemaphoreType.DMA((sectors - 1,)),
            pltpu.SemaphoreType.DMA((sectors - 1,)),
            pltpu.SemaphoreType.DMA((sectors - 1, local)),
            pltpu.SemaphoreType.DMA((sectors - 1, local)),
            pltpu.SemaphoreType.DMA,
            pltpu.SemaphoreType.DMA,
        ],
        compiler_params=pltpu.CompilerParams(
            vmem_limit_bytes=56 * 1024 * 1024, collective_id=0, has_side_effects=True
        ),
    )(
        live_sizes, sector_labels[0], psi_first[0, 0], psi_second[0, 0], left, right_env[0, 0],
        site_tensor[0, 0], left_t, two, one,
    )
    return tuple(out[None, None] for out in outs)


def solution(mesh):
    return jax.shard_map(
        shards,
        mesh=mesh,
        in_specs=(
            P(("groups", "chain"), "sector", None, None),
            P(("groups", "chain"), "sector", None, None),
            P(("groups", "chain"), "sector", None, None),
            P(("groups", "chain"), "sector", None, None),
            P(("groups", "chain"), "sector", None, None),
            P(("groups", "chain"), None, None, None, None),
            P(("groups", "chain"), None, None, None),
            P(("groups", "chain"), None, "sector"),
            P(("groups", "chain"), "sector"),
        ),
        out_specs=(
            P(("groups", "chain"), "sector", None, None),
            P(("groups", "chain"), "sector", None, None),
            P(("groups", "chain"), "sector", None, None),
        ),
        check_vma=False,
    )
```

time: 99.7 us -> 67.5 us (0.68)
  the two profiles are of different devices: /device:TPU:14 before, /device:TPU:0 now
where the time goes in v1:
time: 67.5 us; the launch traced here: 66.9 us
  Pallas kernels  55.9 us (83%)
  local copies, waits for them, and re-layouts  9.5 us (14%)
  between operations  1.41 us (2%)
    pallas_call x1, Pallas kernels, shards(): pl.pallas_call(functools.partial(window_kernel, block, bond, local, secto...  55.9 us
    unnamed x14, local copies, waits for them, and re-layouts  4.7 us
    reshape x2, local copies, waits for them, and re-layouts, padded_operator(): return op.reshape(op.shape[0] * ROWS, op.shape[2] * ROWS)  1.49 us
    another operation x1, local copies, waits for them, and re-layouts, shards(): left.reshape(block, bond, block)  1.37 us

profile of v1, /device:TPU:0, one launch (start us, length us, event | category | flops | bytes accessed | tf_op | source)
XLA Modules:
  0.0 66.9 jit_solution(1924496363536830302)
XLA Ops:
  1.3 0.0 copy-start.4
  1.3 0.6 copy-done.4
  1.9 0.7 %copy.21.labels_ref = s32[26,1]{1,0:T(8,128)} copy(s32[26,1]{0,1:T(1,128)S(1)} %bitcast.39) | data formatting | bytes 208 | tf_op jit(solution)/shard_map/squeeze | solution.py:296
  2.6 1.4 %reshape_squeeze.3 = bf16[64,26,64]{2,1,0:T(8,128)(2,1)S(1)} reshape(bf16[1,1,64,1664]{3,2,1,0:T(8,128)(2,1)} %param.11) | data formatting | bytes 425984 | tf_op jit(solution)/shard_map/reshape;squeeze | solution.py:258
  4.0 1.1 %copy.23 = bf16[64,64,26]{0,2,1:T(8,128)(2,1)S(1)} copy(bf16[64,64,26]{1,2,0:T(8,128)(2,1)S(1)} %bitcast.26) | data formatting | bytes 425984
  5.1 0.1 pad.11.clone
  5.2 0.0 copy-start.3
  5.2 0.0 copy-start
  5.2 0.9 %copy.22.left_t_ref = bf16[64,2048]{1,0:T(8,128)(2,1)} copy(bf16[64,2048]{0,1:T(8,128)(2,1)S(1)} %bitcast.25) | data formatting | bytes 524288 | tf_op jit(solution)/shard_map/reshape | solution.py:259
  6.1 0.0 copy-done.3
  6.2 0.0 copy-done
  6.3 0.1 pad.12
  6.4 0.7 %reshape.29.two_ref = bf16[128,128]{1,0:T(8,128)(2,1)} reshape(bf16[4,32,4,32]{3,2,1,0:T(4,128)(2,1)S(1)} %pad.12) | data formatting | bytes 65536 | tf_op jit(solution)/shard_map/reshape | solution.py:19
  7.1 0.1 pad.13
  7.2 0.7 %reshape.30.one_ref = bf16[128,128]{1,0:T(8,128)(2,1)} reshape(bf16[4,32,4,32]{3,2,1,0:T(4,128)(2,1)S(1)} %pad.13) | data formatting | bytes 65536 | tf_op jit(solution)/shard_map/reshape | solution.py:19
  8.0 55.9 %shard_map.112 = (bf16[64,1024]{1,0:T(8,128)(2,1)}, bf16[64,1024]{1,0:T(8,128)(2,1)}, bf16[64,1664]{1,0:T(8,128)(2,1)}) custom-call(s32[1,1]{1,0:T(1,128)S(6)} %copy.31.live_ref, s32[26,1]{1,0:T(8,128)} %copy.21.labels_ref, bf16[64,1024]{1,0:T(8,128)(2,1)} %bitcast.36, bf16[64,1024]{1,0:T(8,128)(2,1)} %bitcast.37, bf16[64,1664]{1,0:T(8,128)(2,1)} %bitcast.27, ...), custom_call_target="tpu_custom_call" | custom-call | tf_op jit(solution)/shard_map/pallas_call | solution.py:262
  63.9 0.0 copy-start.2
  63.9 0.0 copy-start.1
  63.9 1.6 %copy.32 = bf16[1,1,64,1024]{3,2,1,0:T(8,128)(2,1)} copy(bf16[1,1,64,1024]{3,2,1,0:T(8,128)(2,1)} %bitcast.35) | data formatting | bytes 262144
  65.5 0.0 copy-done.2
  65.5 0.7 copy.33
  66.2 0.0 copy-done.1
  66.2 0.7 %copy.34 = bf16[1,1,64,1664]{3,2,1,0:T(8,128)(2,1)} copy(bf16[1,1,64,1664]{3,2,1,0:T(8,128)(2,1)S(1)} %bitcast.33) | data formatting | bytes 425984
  (6 shorter events, 0.1 us)
Async XLA Ops:
  1.3 0.7 copy-start.4
  5.2 0.9 %copy-start.3 = (s32[1,2,26,26]{3,1,2,0:T(2,128)S(1)}, s32[1,2,26,26]{3,1,2,0:T(2,128)}, u32[]{:S(2)}) copy-start(s32[1,2,26,26]{3,1,2,0:T(2,128)} %param.15) | copy-start | bytes 16228
  5.2 0.9 %copy-start = (bf16[1,2,26,26,16]{3,4,2,1,0:T(8,128)(2,1)S(1)}, bf16[1,2,26,26,16]{3,4,2,1,0:T(8,128)(2,1)}, u32[]{:S(2)}) copy-start(bf16[1,2,26,26,16]{3,4,2,1,0:T(8,128)(2,1)} %param.14) | copy-start | bytes 129796
  63.9 1.6 %copy-start.2 = (bf16[64,1024]{1,0:T(8,128)(2,1)S(1)}, bf16[64,1024]{1,0:T(8,128)(2,1)}, u32[]{:S(2)}) copy-start(bf16[64,1024]{1,0:T(8,128)(2,1)} %get-tuple-element.7) | copy-start | bytes 393220
  63.9 2.3 %copy-start.1 = (bf16[64,1664]{1,0:T(8,128)(2,1)S(1)}, bf16[64,1664]{1,0:T(8,128)(2,1)}, u32[]{:S(2)}) copy-start(bf16[64,1664]{1,0:T(8,128)(2,1)} %get-tuple-element.8) | copy-start | bytes 638980

commit v2 on v1

--- a/solution.py
+++ b/solution.py
@@ -8,6 +8,7 @@
 from jax.sharding import PartitionSpec as P
 
 ROWS = 32
+SKEW = 8
 BF16 = jnp.bfloat16
 F32 = jnp.float32
 MESH = pl.DeviceIdType.MESH
@@ -87,32 +88,34 @@
         a = left_t_ref[:, at].astype(F32)
         for k in range(sectors):
             lk_s[k * block : (k + 1) * block, at] = jnp.where(target == k, a, 0.0).astype(BF16)
-    stride = pair * ROWS
+    stride = pair * ROWS + SKEW
 
     def put(st, w, value):
         x_s[pl.ds(st * ROWS + w, block, stride=stride), :] = value
 
+    for a in range(block):
+        x_s[pl.ds(a * stride + pair * ROWS, SKEW), :] = jnp.zeros((SKEW, wide), F32)
     for st in range(pair):
         for w in range(bond, ROWS):
             put(st, w, jnp.zeros((block, wide), F32))
 
-    def one(st, carry):
-        lhs = psi_s[pl.ds(pl.multiple_of(st * block, block), block), :]
-        for tile in range(bond // 2):
+    together = 4
+    for tile in range(bond // 2):
+        rhs = right_s[pl.ds(tile * 2 * wide, 2 * wide), :]
+        for st in range(0, pair, together):
             got = lax.dot_general(
-                lhs, right_s[pl.ds(tile * 2 * wide, 2 * wide), :], (((1,), (1,)), ((), ())),
+                psi_s[pl.ds(st * block, together * block), :], rhs, (((1,), (1,)), ((), ())),
                 preferred_element_type=F32,
             )
-            put(st, 2 * tile, got[:, :wide])
-            put(st, 2 * tile + 1, got[:, wide:])
-        return carry
-
-    lax.fori_loop(0, pair, one, 0)
+            for i in range(together):
+                put(st + i, 2 * tile, got[i * block : (i + 1) * block, :wide])
+                put(st + i, 2 * tile + 1, got[i * block : (i + 1) * block, wide:])
+
     two = two_ref[...]
     rows = local * ROWS
 
     def middle(a, carry):
-        x = x_s[pl.ds(pl.multiple_of(a * stride, stride), stride), :].astype(BF16)
+        x = x_s[pl.ds(pl.multiple_of(a * stride, SKEW), pair * ROWS), :].astype(BF16)
         x = jnp.concatenate([x[s * rows : (s + 1) * rows] for s in range(local)], axis=1)
         y = jnp.dot(two, x, preferred_element_type=F32).astype(BF16)
         for u in range(local):
@@ -163,7 +166,7 @@
     own = jnp.concatenate([own, own], axis=0)
     op_t = op.astype(F32).T.astype(BF16)
     tiles = local * block // wide
-    env_stride = tiles * rows
+    env_stride = tiles * rows + SKEW
 
     def brought(tile, carry):
         a = left_ref[:, pl.ds(pl.multiple_of(tile * wide, wide), wide)].astype(F32)
@@ -182,7 +185,7 @@
     lax.fori_loop(0, bond // 2, brought, 0)
 
     def closed(e, carry):
-        x = x_s[pl.ds(pl.multiple_of(e * env_stride, env_stride), env_stride), :].astype(BF16)
+        x = x_s[pl.ds(pl.multiple_of(e * env_stride, SKEW), tiles * rows), :].astype(BF16)
         x = jnp.concatenate([x[t * rows : (t + 1) * rows] for t in range(tiles)], axis=1)
         o = jnp.dot(op_t, x, preferred_element_type=F32)
         even = o[:ROWS, :wide]
@@ -271,7 +274,7 @@
         scratch_shapes=[
             pltpu.VMEM((pair * block, wide), BF16),
             pltpu.VMEM((bond * wide, wide), BF16),
-            pltpu.VMEM((block * pair * ROWS, wide), F32),
+            pltpu.VMEM((block * (pair * ROWS + SKEW), wide), F32),
             pltpu.VMEM((local, block * local * ROWS, wide), BF16),
             pltpu.VMEM((block * ROWS, local * wide), BF16),
             pltpu.VMEM((sectors * block, block * ROWS), BF16),

time: 67.5 us -> 55.7 us (0.83)
  Pallas kernels: 55.9 us -> 44.5 us
    pallas_call x1, Pallas kernels: 55.9 us -> 44.5 us  [shards(): pl.pallas_call(functools.partial(window_kernel, block, bond, local, secto...]
where the time goes in v2:
time: 55.7 us; the launch traced here: 55.5 us
  Pallas kernels  44.5 us (80%)
  local copies, waits for them, and re-layouts  9.5 us (17%)
  between operations  1.41 us (3%)
    pallas_call x1, Pallas kernels, shards(): pl.pallas_call(functools.partial(window_kernel, block, bond, local, secto...  44.5 us
    unnamed x14, local copies, waits for them, and re-layouts  4.7 us
    reshape x2, local copies, waits for them, and re-layouts, padded_operator(): return op.reshape(op.shape[0] * ROWS, op.shape[2] * ROWS)  1.49 us
    another operation x1, local copies, waits for them, and re-layouts, shards(): left.reshape(block, bond, block)  1.37 us

profile of v2, /device:TPU:0, one launch (start us, length us, event | category | flops | bytes accessed | tf_op | source)
XLA Modules:
  0.0 55.5 jit_solution(2483009624248332092)
XLA Ops:
  1.3 0.0 copy-start.4
  1.3 0.6 %copy-done.4 = s32[1,26,1]{1,2,0:T(1,128)S(1)} copy-done((s32[1,26,1]{1,2,0:T(1,128)S(1)}, s32[1,26,1]{1,2,0:T(1,128)}, u32[]{:S(2)}) %copy-start.4) | copy-done | bytes 128
  1.9 0.7 %copy.21.labels_ref = s32[26,1]{1,0:T(8,128)} copy(s32[26,1]{0,1:T(1,128)S(1)} %bitcast.39) | data formatting | bytes 208 | tf_op jit(solution)/shard_map/squeeze | solution.py:299
  2.6 1.4 %reshape_squeeze.3 = bf16[64,26,64]{2,1,0:T(8,128)(2,1)S(1)} reshape(bf16[1,1,64,1664]{3,2,1,0:T(8,128)(2,1)} %param.11) | data formatting | bytes 425984 | tf_op jit(solution)/shard_map/reshape;squeeze | solution.py:261
  4.0 1.1 %copy.23 = bf16[64,64,26]{0,2,1:T(8,128)(2,1)S(1)} copy(bf16[64,64,26]{1,2,0:T(8,128)(2,1)S(1)} %bitcast.26) | data formatting | bytes 425984
  5.1 0.1 pad.11.clone
  5.2 0.0 copy-start.3
  5.2 0.0 copy-start
  5.2 0.9 %copy.22.left_t_ref = bf16[64,2048]{1,0:T(8,128)(2,1)} copy(bf16[64,2048]{0,1:T(8,128)(2,1)S(1)} %bitcast.25) | data formatting | bytes 524288 | tf_op jit(solution)/shard_map/reshape | solution.py:262
  6.1 0.0 copy-done.3
  6.2 0.0 copy-done
  6.3 0.1 pad.12
  6.4 0.7 %reshape.29.two_ref = bf16[128,128]{1,0:T(8,128)(2,1)} reshape(bf16[4,32,4,32]{3,2,1,0:T(4,128)(2,1)S(1)} %pad.12) | data formatting | bytes 65536 | tf_op jit(solution)/shard_map/reshape | solution.py:20
  7.1 0.1 pad.13
  7.2 0.7 %reshape.30.one_ref = bf16[128,128]{1,0:T(8,128)(2,1)} reshape(bf16[4,32,4,32]{3,2,1,0:T(4,128)(2,1)S(1)} %pad.13) | data formatting | bytes 65536 | tf_op jit(solution)/shard_map/reshape | solution.py:20
  8.0 44.5 %shard_map.112 = (bf16[64,1024]{1,0:T(8,128)(2,1)}, bf16[64,1024]{1,0:T(8,128)(2,1)}, bf16[64,1664]{1,0:T(8,128)(2,1)}) custom-call(s32[1,1]{1,0:T(1,128)S(6)} %copy.31.live_ref, s32[26,1]{1,0:T(8,128)} %copy.21.labels_ref, bf16[64,1024]{1,0:T(8,128)(2,1)} %bitcast.36, bf16[64,1024]{1,0:T(8,128)(2,1)} %bitcast.37, bf16[64,1664]{1,0:T(8,128)(2,1)} %bitcast.27, ...), custom_call_target="tpu_custom_call" | custom-call | tf_op jit(solution)/shard_map/pallas_call | solution.py:265
  52.5 0.0 copy-start.2
  52.5 0.0 copy-start.1
  52.5 1.6 %copy.32 = bf16[1,1,64,1024]{3,2,1,0:T(8,128)(2,1)} copy(bf16[1,1,64,1024]{3,2,1,0:T(8,128)(2,1)} %bitcast.35) | data formatting | bytes 262144
  54.1 0.0 copy-done.2
  54.1 0.7 %copy.33 = bf16[1,1,64,1024]{3,2,1,0:T(8,128)(2,1)} copy(bf16[1,1,64,1024]{3,2,1,0:T(8,128)(2,1)S(1)} %bitcast.34) | data formatting | bytes 262144
  54.8 0.0 copy-done.1
  54.8 0.7 %copy.34 = bf16[1,1,64,1664]{3,2,1,0:T(8,128)(2,1)} copy(bf16[1,1,64,1664]{3,2,1,0:T(8,128)(2,1)S(1)} %bitcast.33) | data formatting | bytes 425984
  (6 shorter events, 0.1 us)
Async XLA Ops:
  1.3 0.7 %copy-start.4 = (s32[1,26,1]{1,2,0:T(1,128)S(1)}, s32[1,26,1]{1,2,0:T(1,128)}, u32[]{:S(2)}) copy-start(s32[1,26,1]{1,2,0:T(1,128)} %param.16) | copy-start | bytes 316
  5.2 0.9 %copy-start.3 = (s32[1,2,26,26]{3,1,2,0:T(2,128)S(1)}, s32[1,2,26,26]{3,1,2,0:T(2,128)}, u32[]{:S(2)}) copy-start(s32[1,2,26,26]{3,1,2,0:T(2,128)} %param.15) | copy-start | bytes 16228
  5.2 0.9 %copy-start = (bf16[1,2,26,26,16]{3,4,2,1,0:T(8,128)(2,1)S(1)}, bf16[1,2,26,26,16]{3,4,2,1,0:T(8,128)(2,1)}, u32[]{:S(2)}) copy-start(bf16[1,2,26,26,16]{3,4,2,1,0:T(8,128)(2,1)} %param.14) | copy-start | bytes 129796
  52.5 1.6 %copy-start.2 = (bf16[64,1024]{1,0:T(8,128)(2,1)S(1)}, bf16[64,1024]{1,0:T(8,128)(2,1)}, u32[]{:S(2)}) copy-start(bf16[64,1024]{1,0:T(8,128)(2,1)} %get-tuple-element.7) | copy-start | bytes 393220
  52.5 2.3 %copy-start.1 = (bf16[64,1664]{1,0:T(8,128)(2,1)S(1)}, bf16[64,1664]{1,0:T(8,128)(2,1)}, u32[]{:S(2)}) copy-start(bf16[64,1664]{1,0:T(8,128)(2,1)} %get-tuple-element.8) | copy-start | bytes 638980

commit v3 on v2

--- a/solution.py
+++ b/solution.py
@@ -8,7 +8,7 @@
 from jax.sharding import PartitionSpec as P
 
 ROWS = 32
-SKEW = 8
+SKEW = 9
 BF16 = jnp.bfloat16
 F32 = jnp.float32
 MESH = pl.DeviceIdType.MESH
@@ -115,7 +115,7 @@
     rows = local * ROWS
 
     def middle(a, carry):
-        x = x_s[pl.ds(pl.multiple_of(a * stride, SKEW), pair * ROWS), :].astype(BF16)
+        x = x_s[pl.ds(a * stride, pair * ROWS), :].astype(BF16)
         x = jnp.concatenate([x[s * rows : (s + 1) * rows] for s in range(local)], axis=1)
         y = jnp.dot(two, x, preferred_element_type=F32).astype(BF16)
         for u in range(local):
@@ -125,9 +125,9 @@
                 ]
         return carry
 
-    lax.fori_loop(0, block, middle, 0, unroll=2)
+    lax.fori_loop(0, block, middle, 0, unroll=4)
     op = one_ref[...]
-    group = 4
+    group = 8
 
     def sum_copy(j, u):
         return pltpu.make_async_remote_copy(
@@ -182,10 +182,10 @@
                     ]
         return carry
 
-    lax.fori_loop(0, bond // 2, brought, 0)
+    lax.fori_loop(0, bond // 2, brought, 0, unroll=True)
 
     def closed(e, carry):
-        x = x_s[pl.ds(pl.multiple_of(e * env_stride, SKEW), tiles * rows), :].astype(BF16)
+        x = x_s[pl.ds(e * env_stride, tiles * rows), :].astype(BF16)
         x = jnp.concatenate([x[t * rows : (t + 1) * rows] for t in range(tiles)], axis=1)
         o = jnp.dot(op_t, x, preferred_element_type=F32)
         even = o[:ROWS, :wide]

time: 55.7 us -> 51 us (0.916)
  Pallas kernels: 44.5 us -> 39.8 us
    pallas_call x1, Pallas kernels: 44.5 us -> 39.8 us  [shards(): pl.pallas_call(functools.partial(window_kernel, block, bond, local, secto...]
where the time goes in v3:
time: 51 us; the launch traced here: 50.8 us
  Pallas kernels  39.8 us (78%)
  local copies, waits for them, and re-layouts  9.5 us (19%)
  between operations  1.41 us (3%)
    pallas_call x1, Pallas kernels, shards(): pl.pallas_call(functools.partial(window_kernel, block, bond, local, secto...  39.8 us
    unnamed x14, local copies, waits for them, and re-layouts  4.7 us
    reshape x2, local copies, waits for them, and re-layouts, padded_operator(): return op.reshape(op.shape[0] * ROWS, op.shape[2] * ROWS)  1.49 us
    another operation x1, local copies, waits for them, and re-layouts, shards(): left.reshape(block, bond, block)  1.37 us

profile of v3, /device:TPU:0, one launch (start us, length us, event | category | flops | bytes accessed | tf_op | source)
XLA Modules:
  0.0 50.8 jit_solution(13429687914960382467)
XLA Ops:
  1.3 0.0 copy-start.4
  1.3 0.6 %copy-done.4 = s32[1,26,1]{1,2,0:T(1,128)S(1)} copy-done((s32[1,26,1]{1,2,0:T(1,128)S(1)}, s32[1,26,1]{1,2,0:T(1,128)}, u32[]{:S(2)}) %copy-start.4) | copy-done | bytes 128
  1.9 0.7 %copy.21.labels_ref = s32[26,1]{1,0:T(8,128)} copy(s32[26,1]{0,1:T(1,128)S(1)} %bitcast.39) | data formatting | bytes 208 | tf_op jit(solution)/shard_map/squeeze | solution.py:299
  2.6 1.4 %reshape_squeeze.3 = bf16[64,26,64]{2,1,0:T(8,128)(2,1)S(1)} reshape(bf16[1,1,64,1664]{3,2,1,0:T(8,128)(2,1)} %param.11) | data formatting | bytes 425984 | tf_op jit(solution)/shard_map/reshape;squeeze | solution.py:261
  4.0 1.1 %copy.23 = bf16[64,64,26]{0,2,1:T(8,128)(2,1)S(1)} copy(bf16[64,64,26]{1,2,0:T(8,128)(2,1)S(1)} %bitcast.26) | data formatting | bytes 425984
  5.1 0.1 pad.11.clone
  5.2 0.0 copy-start.3
  5.2 0.0 copy-start
  5.2 0.9 %copy.22.left_t_ref = bf16[64,2048]{1,0:T(8,128)(2,1)} copy(bf16[64,2048]{0,1:T(8,128)(2,1)S(1)} %bitcast.25) | data formatting | bytes 524288 | tf_op jit(solution)/shard_map/reshape | solution.py:262
  6.1 0.0 copy-done.3
  6.2 0.0 copy-done
  6.3 0.1 pad.12
  6.4 0.7 %reshape.29.two_ref = bf16[128,128]{1,0:T(8,128)(2,1)} reshape(bf16[4,32,4,32]{3,2,1,0:T(4,128)(2,1)S(1)} %pad.12) | data formatting | bytes 65536 | tf_op jit(solution)/shard_map/reshape | solution.py:20
  7.1 0.1 pad.13
  7.2 0.7 %reshape.30.one_ref = bf16[128,128]{1,0:T(8,128)(2,1)} reshape(bf16[4,32,4,32]{3,2,1,0:T(4,128)(2,1)S(1)} %pad.13) | data formatting | bytes 65536 | tf_op jit(solution)/shard_map/reshape | solution.py:20
  8.0 39.8 %shard_map.112 = (bf16[64,1024]{1,0:T(8,128)(2,1)}, bf16[64,1024]{1,0:T(8,128)(2,1)}, bf16[64,1664]{1,0:T(8,128)(2,1)}) custom-call(s32[1,1]{1,0:T(1,128)S(6)} %copy.31.live_ref, s32[26,1]{1,0:T(8,128)} %copy.21.labels_ref, bf16[64,1024]{1,0:T(8,128)(2,1)} %bitcast.36, bf16[64,1024]{1,0:T(8,128)(2,1)} %bitcast.37, bf16[64,1664]{1,0:T(8,128)(2,1)} %bitcast.27, ...), custom_call_target="tpu_custom_call" | custom-call | tf_op jit(solution)/shard_map/pallas_call | solution.py:265
  47.8 0.0 copy-start.2
  47.8 0.0 copy-start.1
  47.8 1.6 %copy.32 = bf16[1,1,64,1024]{3,2,1,0:T(8,128)(2,1)} copy(bf16[1,1,64,1024]{3,2,1,0:T(8,128)(2,1)} %bitcast.35) | data formatting | bytes 262144
  49.4 0.0 copy-done.2
  49.4 0.7 %copy.33 = bf16[1,1,64,1024]{3,2,1,0:T(8,128)(2,1)} copy(bf16[1,1,64,1024]{3,2,1,0:T(8,128)(2,1)S(1)} %bitcast.34) | data formatting | bytes 262144
  50.1 0.0 copy-done.1
  50.1 0.7 %copy.34 = bf16[1,1,64,1664]{3,2,1,0:T(8,128)(2,1)} copy(bf16[1,1,64,1664]{3,2,1,0:T(8,128)(2,1)S(1)} %bitcast.33) | data formatting | bytes 425984
  (6 shorter events, 0.1 us)
Async XLA Ops:
  1.3 0.7 %copy-start.4 = (s32[1,26,1]{1,2,0:T(1,128)S(1)}, s32[1,26,1]{1,2,0:T(1,128)}, u32[]{:S(2)}) copy-start(s32[1,26,1]{1,2,0:T(1,128)} %param.16) | copy-start | bytes 316
  5.2 0.9 %copy-start.3 = (s32[1,2,26,26]{3,1,2,0:T(2,128)S(1)}, s32[1,2,26,26]{3,1,2,0:T(2,128)}, u32[]{:S(2)}) copy-start(s32[1,2,26,26]{3,1,2,0:T(2,128)} %param.15) | copy-start | bytes 16228
  5.2 0.9 %copy-start = (bf16[1,2,26,26,16]{3,4,2,1,0:T(8,128)(2,1)S(1)}, bf16[1,2,26,26,16]{3,4,2,1,0:T(8,128)(2,1)}, u32[]{:S(2)}) copy-start(bf16[1,2,26,26,16]{3,4,2,1,0:T(8,128)(2,1)} %param.14) | copy-start | bytes 129796
  47.8 1.6 %copy-start.2 = (bf16[64,1024]{1,0:T(8,128)(2,1)S(1)}, bf16[64,1024]{1,0:T(8,128)(2,1)}, u32[]{:S(2)}) copy-start(bf16[64,1024]{1,0:T(8,128)(2,1)} %get-tuple-element.7) | copy-start | bytes 393220
  47.8 2.3 %copy-start.1 = (bf16[64,1664]{1,0:T(8,128)(2,1)S(1)}, bf16[64,1664]{1,0:T(8,128)(2,1)}, u32[]{:S(2)}) copy-start(bf16[64,1664]{1,0:T(8,128)(2,1)} %get-tuple-element.8) | copy-start | bytes 638980
